TPU v7x, 256 devices: a whole 4x4x8 slice. The times are simulated.
256 devices in a mesh: row: 16 (over x, y_hi, core), col: 16 (over y_lo, z).
Axes of the slice: x: 4, y: 4 (y_hi: 2, y_lo: 2; y = y_hi * 2 + y_lo), z: 8, core: 2. Of those that a mesh axis runs over, the one named last changes fastest.
Arguments:
- matrix: float32 [16, 3, 256, 16, 3, 256], P('row', None, None, 'col'), as said below
- checksum: float32 [16, 3, 256, 3, 256], P('row'), as said below
- failed: int32 [16], P('col'), may hold values from 0 to 15, as said below
Outputs:
- factored: float32 [16, 3, 256, 16, 3, 256], P('row', None, None, 'col')
- updated_checksum_result: float32 [16, 3, 256, 3, 256], P('row')
Inputs may be any that keep to these rules, and one draw needn't show every extreme that they name: `failed`: a permutation of the grid column indices; entry 0 names the grid column whose tiles in matrix carry no information. With the lost grid column rebuilt from checksum, matrix is symmetric positive definite. `checksum`: for each grid row, the sum over all grid columns of the intact matrix's tiles, the lost column included.
All inputs are finite; a program needn't handle non-finite values.
Results may differ from a plain program's by a relative error of at most 0.0003.
Values sent between devices are 32-bit elements; how exact they have to be, the bound alone decides.
No kernel may reach another device: no remote copies, remote signals or barrier semaphores. Data moves between devices by JAX's collectives and lax.ppermute only.
A program may use at most 128 MiB of HBM per device.

v0:
```python
import jax
import jax.numpy as jnp
from jax import lax
from jax.sharding import Mesh
from jax.sharding import PartitionSpec as P

PANELS = 3
COL = ("col_0", "col_1")


def from_root(x, axis, root):
    return lax.dynamic_index_in_dim(lax.all_gather(x, axis), root, 0, keepdims=False)


def copy_for_each(x, axis):
    peers = lax.axis_size(axis)
    return lax.all_to_all(jnp.broadcast_to(x[None], (peers, *x.shape)), axis, 0, 0, tiled=True)


def joined_along(tiles, dim):
    tiles = jnp.moveaxis(tiles, 0, dim)
    shape = tiles.shape
    return tiles.reshape(*shape[:dim], shape[dim] * shape[dim + 1], *shape[dim + 2 :])


def collect(x, axis, dim):
    tiles = copy_for_each(x, axis)
    return joined_along(tiles, dim)


def from_root_2(x, axes, root):
    x = jnp.where(lax.axis_index(axes) == root, x, jnp.zeros_like(x))
    for axis in axes:
        x = lax.psum(x, axis)
    return x


def solve_panel(column, factor, row_tiles, panel):
    tile_count, width = (column.shape[0], column.shape[1])
    stacked = column.reshape(tile_count * width, width)
    solved = jax.scipy.linalg.solve_triangular(factor, stacked.T, lower=True).T.reshape(
        tile_count, width, width
    )
    chosen = jnp.where((row_tiles > panel)[:, None, None], solved, 0.0)
    return jnp.where((row_tiles == panel)[:, None, None], factor[None, :, :], chosen)


def matching_tiles(panel_rows, column_position, rows_count):
    width = panel_rows.shape[1]
    source = (column_position + 0) % rows_count
    received = [from_root(panel_rows, "row", source)]
    return jnp.stack(received, axis=1).reshape(-1, width, width)


def shards(matrix, checksum, failed):
    rows_count = lax.axis_size("row")
    cols_count = lax.axis_size(COL)
    row_index = lax.axis_index("row")
    column_position = lax.axis_index(COL)
    tile_rows, width, tile_cols = (matrix.shape[1], matrix.shape[2], matrix.shape[4])
    resident_tiles = matrix.reshape(tile_rows, width, tile_cols, width)
    totals = checksum.reshape(tile_rows, width, tile_cols, width)
    missing_tiles = collect(failed, COL, 0)[0]
    healthy_member = jnp.where(column_position != missing_tiles, resident_tiles, 0.0)
    remaining_peers = lax.psum(healthy_member, COL)
    work = jnp.where(column_position == missing_tiles, totals - remaining_peers, resident_tiles)
    row_tiles = row_index + jnp.arange(tile_rows, dtype=jnp.int32) * rows_count
    col_tiles = column_position + jnp.arange(tile_cols, dtype=jnp.int32) * cols_count
    identity = jnp.eye(width, dtype=jnp.float32)
    finished = []
    for panel in range(PANELS):
        col_root = panel % cols_count
        col_slot = panel // cols_count
        row_root = panel % rows_count
        row_slot = panel // rows_count
        column = work[:, :, col_slot, :]
        owner = jnp.logical_and(row_index == row_root, column_position == col_root)
        diag_input = jnp.where(owner, work[row_slot, :, col_slot, :], identity)
        factor_here = jnp.linalg.cholesky(diag_input)
        factor = from_root(factor_here, "row", row_root)
        own_rows = solve_panel(column, factor, row_tiles, panel)
        panel_rows = from_root_2(own_rows, COL, col_root)
        panel_cols = matching_tiles(panel_rows, column_position, rows_count)
        update = jnp.einsum(
            "axr,byr->axby", panel_rows, panel_cols, precision=lax.Precision.HIGHEST
        )
        work = work - update
        finished.append((col_root, col_slot, panel_rows))
    totals = lax.psum(work, COL)
    for col_root, col_slot, panel_rows in finished:
        current = work[:, :, col_slot, :]
        work = work.at[:, :, col_slot, :].set(
            jnp.where(column_position == col_root, panel_rows, current)
        )
    keep = (row_tiles[:, None] >= col_tiles[None, :])[:, None, :, None]
    factored = jnp.where(keep, work, 0.0).reshape(matrix.shape)
    return (factored, totals.reshape(checksum.shape))


def solution(mesh):
    finer = Mesh(mesh.devices.reshape(mesh.shape["row"], 2, 8), ("row", "col_0", "col_1"))
    in_specs = (P("row", None, None, COL, None, None), P("row", None, None, None, None), P(COL))
    out_specs = (P("row", None, None, COL, None, None), P("row", None, None, None, None))
    return jax.shard_map(
        shards, mesh=finer, in_specs=in_specs, out_specs=out_specs, check_vma=False
    )
```

profile of v0, /device:TPU:30, one launch (start us, length us, event | category | flops | bytes accessed | tf_op | source)
XLA Modules:
  0.0 1397.2 jit_solution(1693049435501583578)
XLA Ops:
  8.4 9.9 all-to-all-start
  18.4 5.5 copy.59
  23.9 1.5 all-to-all-done
  26.7 1.7 bitcast_select_fusion.1
  28.4 3.0 copy.58
  32.2 138.1 %all-reduce.10.cloned.1.call-done = f32[3,256,3,256]{1,3,2,0:T(8,128)} async-done(((f32[3,256,3,256]{1,3,2,0:T(8,128)}), f32[3,256,3,256]{1,3,2,0:T(8,128)}) %all-reduce.10.cloned.1.call-update) | async-done | bytes 2359312 | tf_op jit(solution)/shard_map/psum | solution.py:65
  170.3 2.8 bitcast_select_fusion
  173.1 1.4 copy-done.1
  174.7 1.1 fusion.18
  175.8 11.7 cholesky.172
  187.5 9.8 custom-call.15
  197.9 11.7 cholesky.189
  213.3 56.5 %all-gather.13.cloned.1.call-done = f32[4096,256]{1,0:T(8,128)} async-done(((f32[256,256]{1,0:T(8,128)}), f32[4096,256]{1,0:T(8,128)}) %all-gather.13.cloned.1.call-update) | async-done | bytes 4194320 | tf_op jit(solution)/shard_map/all_gather | solution.py:12
  271.0 4.1 while.9
  271.7 1.4 bitcast_dynamic-update-slice_fusion.9
  273.7 1.4 bitcast_dynamic-update-slice_fusion.9
  275.2 19.7 %custom-call.16 = f32[2,128,128]{1,2,0:T(8,128)S(1)} custom-call(f32[2,128,128]{2,1,0:T(8,128)S(1)} %get-tuple-element.60), custom_call_target="InvertDiagBlocksLowerTriangular" | custom-call | tf_op jit(solution)/shard_map/jit(_solve_triangular)/triangular_solve | solution.py:41
  297.0 1.0 select_select_fusion.2
  298.1 46.3 %all-reduce.12.cloned.1.call-done = f32[3,256,256]{1,2,0:T(8,128)} async-done(((f32[3,256,256]{1,2,0:T(8,128)}), f32[3,256,256]{1,2,0:T(8,128)}) %all-reduce.12.cloned.1.call-update) | async-done | bytes 786448 | tf_op jit(solution)/shard_map/psum | solution.py:34
  344.4 78.6 %all-reduce.14.cloned.1.call-done = f32[3,256,256]{1,2,0:T(8,128)} async-done(((f32[3,256,256]{1,2,0:T(8,128)}), f32[3,256,256]{1,2,0:T(8,128)}) %all-reduce.14.cloned.1.call-update) | async-done | bytes 786448 | tf_op jit(solution)/shard_map/psum | solution.py:34
  423.1 2.4 copy.66
  425.5 91.6 %all-gather.15.cloned.1.call-done = f32[48,256,256]{2,1,0:T(8,128)} async-done(((f32[3,256,256]{2,1,0:T(8,128)}), f32[48,256,256]{2,1,0:T(8,128)}) %all-gather.15.cloned.1.call-update) | async-done | bytes 12582928 | tf_op jit(solution)/shard_map/all_gather | solution.py:12
  517.2 4.1 convolution_subtract_fusion.2
  521.5 11.7 cholesky.206
  533.9 9.8 custom-call.17
  544.2 24.1 %cholesky.223 = f32[128,128]{1,0:T(8,128)S(1)} custom-call(f32[128,128]{1,0:T(8,128)S(1)} %convolution_subtract_fusion.7), custom_call_target="Cholesky" | custom-call | tf_op jit(solution)/shard_map/jit(cholesky)/cholesky | solution.py:79
  571.1 1.1 copy.71
  572.3 1.4 copy.72
  573.7 58.0 %all-gather.17.cloned.1.call-done = f32[4096,256]{1,0:T(8,128)} async-done(((f32[256,256]{1,0:T(8,128)}), f32[4096,256]{1,0:T(8,128)}) %all-gather.17.cloned.1.call-update) | async-done | bytes 4194320 | tf_op jit(solution)/shard_map/all_gather | solution.py:12
  631.7 1.7 fusion.46
  633.4 1.8 copy.70
  635.2 4.1 while.10
  635.8 1.4 bitcast_dynamic-update-slice_fusion.10
  637.8 1.4 bitcast_dynamic-update-slice_fusion.10
  639.2 20.3 %custom-call.18 = f32[2,128,128]{1,2,0:T(8,128)} custom-call(f32[2,128,128]{2,1,0:T(8,128)S(1)} %get-tuple-element.61), custom_call_target="InvertDiagBlocksLowerTriangular" | custom-call | tf_op jit(solution)/shard_map/jit(_solve_triangular)/triangular_solve | solution.py:41
  659.5 1.4 fusion.12
  661.4 1.4 fusion.27
  662.8 1.1 copy.73
  664.0 1.4 copy.74
  666.5 46.3 %all-reduce.16.cloned.1.call-done = f32[3,256,256]{1,2,0:T(8,128)} async-done(((f32[3,256,256]{1,2,0:T(8,128)}), f32[3,256,256]{1,2,0:T(8,128)}) %all-reduce.16.cloned.1.call-update) | async-done | bytes 786448 | tf_op jit(solution)/shard_map/psum | solution.py:34
  712.8 78.8 %all-reduce.18.cloned.1.call-done = f32[3,256,256]{1,2,0:T(8,128)} async-done(((f32[3,256,256]{1,2,0:T(8,128)}), f32[3,256,256]{1,2,0:T(8,128)}) %all-reduce.18.cloned.1.call-update) | async-done | bytes 786448 | tf_op jit(solution)/shard_map/psum | solution.py:34
  791.6 2.4 copy.75
  794.1 91.8 %all-gather.19.cloned.1.call-done = f32[48,256,256]{2,1,0:T(8,128)} async-done(((f32[3,256,256]{2,1,0:T(8,128)}), f32[48,256,256]{2,1,0:T(8,128)}) %all-gather.19.cloned.1.call-update) | async-done | bytes 12582928 | tf_op jit(solution)/shard_map/all_gather | solution.py:12
  885.9 3.4 convolution_subtract_fusion.1
  889.3 1.4 copy-done
  890.9 1.1 fusion.16
  892.0 11.7 cholesky.240
  904.4 9.8 custom-call.19
  914.7 11.9 cholesky.257
  930.1 60.1 %all-gather.21.cloned.1.call-done = f32[4096,256]{1,0:T(8,128)} async-done(((f32[256,256]{1,0:T(8,128)}), f32[4096,256]{1,0:T(8,128)}) %all-gather.21.cloned.1.call-update) | async-done | bytes 4194320 | tf_op jit(solution)/shard_map/all_gather | solution.py:12
  991.3 4.1 while.11
  991.9 1.4 bitcast_dynamic-update-slice_fusion.11
  994.0 1.4 bitcast_dynamic-update-slice_fusion.11
  995.4 19.7 %custom-call.20 = f32[2,128,128]{1,2,0:T(8,128)S(1)} custom-call(f32[2,128,128]{2,1,0:T(8,128)S(1)} %get-tuple-element.62), custom_call_target="InvertDiagBlocksLowerTriangular" | custom-call | tf_op jit(solution)/shard_map/jit(_solve_triangular)/triangular_solve | solution.py:41
  1018.3 46.3 %all-reduce.20.cloned.1.call-done = f32[3,256,256]{1,2,0:T(8,128)} async-done(((f32[3,256,256]{1,2,0:T(8,128)}), f32[3,256,256]{1,2,0:T(8,128)}) %all-reduce.20.cloned.1.call-update) | async-done | bytes 786448 | tf_op jit(solution)/shard_map/psum | solution.py:34
  1064.7 78.6 %all-reduce.22.cloned.1.call-done = f32[3,256,256]{1,2,0:T(8,128)} async-done(((f32[3,256,256]{1,2,0:T(8,128)}), f32[3,256,256]{1,2,0:T(8,128)}) %all-reduce.22.cloned.1.call-update) | async-done | bytes 786448 | tf_op jit(solution)/shard_map/psum | solution.py:34
  1143.3 2.4 copy.84
  1145.7 91.8 %all-gather.23.cloned.1.call-done = f32[48,256,256]{2,1,0:T(8,128)} async-done(((f32[3,256,256]{2,1,0:T(8,128)}), f32[48,256,256]{2,1,0:T(8,128)}) %all-gather.23.cloned.1.call-update) | async-done | bytes 12582928 | tf_op jit(solution)/shard_map/all_gather | solution.py:12
  1237.6 4.1 convolution_subtract_fusion
  1241.6 1.4 copy.142
  1245.6 1.7 select_bitcast_fusion
  1247.3 6.6 copy.90
  1253.9 133.3 %all-reduce.24.cloned.1.call-done = f32[1,3,256,3,256]{2,4,3,1,0:T(8,128)} async-done(((f32[1,3,256,3,256]{2,4,3,1,0:T(8,128)}), f32[1,3,256,3,256]{2,4,3,1,0:T(8,128)}) %all-reduce.24.cloned.1.call-update) | async-done | bytes 2359312 | tf_op jit(solution)/shard_map/psum | solution.py:89
  1387.2 3.0 copy.91
  (135 shorter events, 26.3 us)
Async XLA Ops:
  8.4 17.0 %all-to-all-start = ((s32[16,1,1]{2,1,0:T(1,128)}), s32[16,1,1]{2,1,0:T(1,128)S(1)}, u32[]{:S(2)}, u32[]{:S(2)}) async-start(s32[16,1,1]{2,1,0:T(1,128)} %broadcast_in_dim.103), calls=%async_computation | async-start | bytes 16384 | tf_op jit(solution)/shard_map/all_to_all | solution.py:17
  18.4 151.9 %all-reduce.10.cloned.1.call-start = ((), (), s32[]{:S(2)}) async-start(), calls=%async_computation.1 | async-start | bytes 4718592 | tf_op jit(solution)/shard_map/psum | solution.py:65
  28.4 241.4 %all-gather.13.cloned.1.call-start = ((), (), s32[]{:S(2)}) async-start(), calls=%async_computation.9 | async-start | bytes 4456448 | tf_op jit(solution)/shard_map/all_gather | solution.py:12
  173.1 1.4 copy-start.1
  174.6 38.2 %slice-start.1 = ((f32[3,256,3,256]{1,3,2,0:T(8,128)}), f32[3,256,1,256]{1,3,2,0:T(8,128)S(1)}, s32[]{:S(2)}) async-start(f32[3,256,3,256]{1,3,2,0:T(8,128)} %copy-done.1), calls=%async_computation.16 | async-start | bytes 1572864 | tf_op jit(solution)/shard_map/slice | solution.py:76
  212.4 131.9 %all-reduce.12.cloned.1.call-start = ((), (), s32[]{:S(2)}) async-start(), calls=%async_computation.2 | async-start | bytes 1572864 | tf_op jit(solution)/shard_map/psum | solution.py:34
  298.0 125.0 %all-reduce.14.cloned.1.call-start = ((), (), s32[]{:S(2)}) async-start(), calls=%async_computation.3 | async-start | bytes 1572864 | tf_op jit(solution)/shard_map/psum | solution.py:34
  344.4 172.8 %all-gather.15.cloned.1.call-start = ((), (), s32[]{:S(2)}) async-start(), calls=%async_computation.10 | async-start | bytes 13369344 | tf_op jit(solution)/shard_map/all_gather | solution.py:12
  423.1 94.1 %copy-start.4 = (f32[3,256,256]{1,2,0:T(8,128)S(1)}, f32[3,256,256]{1,2,0:T(8,128)}, u32[]{:S(2)}) copy-start(f32[3,256,256]{1,2,0:T(8,128)} %all-reduce.14.cloned.1.call-done) | copy-start | bytes 2359300
  425.4 206.2 %all-gather.17.cloned.1.call-start = ((), (), s32[]{:S(2)}) async-start(), calls=%async_computation.11 | async-start | bytes 4456448 | tf_op jit(solution)/shard_map/all_gather | solution.py:12
  571.0 141.8 %all-reduce.16.cloned.1.call-start = ((), (), s32[]{:S(2)}) async-start(), calls=%async_computation.4 | async-start | bytes 1572864 | tf_op jit(solution)/shard_map/psum | solution.py:34
  662.7 2.6 copy-start.8
  666.4 125.2 %all-reduce.18.cloned.1.call-start = ((), (), s32[]{:S(2)}) async-start(), calls=%async_computation.5 | async-start | bytes 1572864 | tf_op jit(solution)/shard_map/psum | solution.py:34
  712.8 173.1 %all-gather.19.cloned.1.call-start = ((), (), s32[]{:S(2)}) async-start(), calls=%async_computation.12 | async-start | bytes 13369344 | tf_op jit(solution)/shard_map/all_gather | solution.py:12
  791.6 94.3 %copy-start.2 = (f32[3,256,256]{1,2,0:T(8,128)S(1)}, f32[3,256,256]{1,2,0:T(8,128)}, u32[]{:S(2)}) copy-start(f32[3,256,256]{1,2,0:T(8,128)} %all-reduce.18.cloned.1.call-done) | copy-start | bytes 2359300
  794.0 196.1 %all-gather.21.cloned.1.call-start = ((), (), s32[]{:S(2)}) async-start(), calls=%async_computation.13 | async-start | bytes 4456448 | tf_op jit(solution)/shard_map/all_gather | solution.py:12
  889.3 1.4 copy-start
  890.8 38.8 %slice-start = ((f32[3,256,3,256]{1,3,2,0:T(8,128)}), f32[3,256,1,256]{1,3,2,0:T(8,128)S(1)}, s32[]{:S(2)}) async-start(f32[3,256,3,256]{1,3,2,0:T(8,128)} %copy-done), calls=%async_computation.15 | async-start | bytes 1572864 | tf_op jit(solution)/shard_map/slice | solution.py:76
  929.5 135.1 %all-reduce.20.cloned.1.call-start = ((), (), s32[]{:S(2)}) async-start(), calls=%async_computation.6 | async-start | bytes 1572864 | tf_op jit(solution)/shard_map/psum | solution.py:34
  1018.3 125.0 %all-reduce.22.cloned.1.call-start = ((), (), s32[]{:S(2)}) async-start(), calls=%async_computation.7 | async-start | bytes 1572864 | tf_op jit(solution)/shard_map/psum | solution.py:34
  1064.6 172.9 %all-gather.23.cloned.1.call-start = ((), (), s32[]{:S(2)}) async-start(), calls=%async_computation.14 | async-start | bytes 13369344 | tf_op jit(solution)/shard_map/all_gather | solution.py:12
  1143.3 94.2 %copy-start.6 = (f32[3,256,256]{1,2,0:T(8,128)S(1)}, f32[3,256,256]{1,2,0:T(8,128)}, u32[]{:S(2)}) copy-start(f32[3,256,256]{1,2,0:T(8,128)} %all-reduce.22.cloned.1.call-done) | copy-start | bytes 2359300
  1145.7 241.5 %all-reduce.24.cloned.1.call-start = ((), (), s32[]{:S(2)}) async-start(), calls=%async_computation.8 | async-start | bytes 4718592 | tf_op jit(solution)/shard_map/psum | solution.py:89
  1243.0 1.1 copy-start.5
  1243.1 1.4 copy-start.3
  1244.3 1.2 copy-start.7
Sparse Core Ops, SparseCore 0:
  28.5 141.7 all-reduce.9
  212.6 57.2 all-gather.12
  298.2 46.1 all-reduce.11
  346.7 76.3 all-reduce.13
  426.2 90.9 all-gather.14
  571.1 60.5 all-gather.16
  666.6 46.1 all-reduce.15
  715.2 76.3 all-reduce.17
  794.9 90.9 all-gather.18
  929.6 60.5 all-gather.20
  1018.4 46.1 all-reduce.19
  1066.9 76.3 all-reduce.21
  1146.6 90.9 all-gather.22
  1243.2 143.9 all-reduce.23
where the time goes:
time: 1410 us; the launch traced here: 1400 us
  waiting for transfers between devices  1100 us (78%)
  other arithmetic  194 us (14%)
  local copies, waits for them, and re-layouts  54.7 us (4%)
  between operations  21 us (1%)
  matrix products  19.2 us (1%)
    all_gather x6, waiting for transfers between devices, from_root(): lax.all_gather(x, axis)  450 us
    psum x6, waiting for transfers between devices, from_root_2(): x = lax.psum(x, axis)  375 us
    psum x1, waiting for transfers between devices, shards(): remaining_peers = lax.psum(healthy_member, COL)  138 us
    psum x1, waiting for transfers between devices, shards(): totals = lax.psum(work, COL)  133 us
    another operation x20, other arithmetic, shards(): factor_here = jnp.linalg.cholesky(diag_input)  116 us
    another operation x4, other arithmetic, solve_panel(): jax.scipy.linalg.solve_triangular(factor, stacked.T, lower=True)  59.7 us
  transfers between devices with their start and end apart: 15, of which 15 were waited for; matrix products, arithmetic and copies ran while one was open for 2% of the time, Pallas kernels for 0%

commit v1 on v0

v1 whole, which is shorter than its diff:
```python
import jax
import jax.numpy as jnp
from jax import lax
from jax.sharding import Mesh
from jax.sharding import PartitionSpec as P

PANELS = 3
COL = ("col_0", "col_1")
HIGHEST = lax.Precision.HIGHEST


def gather_by_exchange(x, axis):
    peers = lax.axis_size(axis)
    return lax.all_to_all(jnp.broadcast_to(x[None], (peers, *x.shape)), axis, 0, 0, tiled=True)


def mm(a, b):
    return jnp.dot(a, b, precision=HIGHEST)


def mm_t(a, b):
    return lax.dot_general(a, b, (((1,), (1,)), ((), ())), precision=HIGHEST)


def factor_lead(lead, width):
    eye = jnp.eye(width, dtype=jnp.float32)
    tile = lambda i, j: lead[i * width : (i + 1) * width, j * width : (j + 1) * width]
    blocks = {(i, j): tile(i, j) for i in range(PANELS) for j in range(i + 1)}
    inverses = []
    for k in range(PANELS):
        factor = jnp.linalg.cholesky(blocks[k, k])
        inverse = jax.scipy.linalg.solve_triangular(factor, eye, lower=True)
        inverses.append(inverse)
        for i in range(k + 1, PANELS):
            blocks[i, k] = mm_t(blocks[i, k], inverse)
        for i in range(k + 1, PANELS):
            for j in range(k + 1, i + 1):
                blocks[i, j] = blocks[i, j] - mm_t(blocks[i, k], blocks[j, k])
    return blocks, inverses


def solve_rows(rows, blocks, inverses, width):
    out = []
    for k in range(PANELS):
        part = rows[:, k * width : (k + 1) * width]
        for m in range(k):
            part = part - mm_t(out[m], blocks[k, m])
        out.append(mm_t(part, inverses[k]))
    return jnp.concatenate(out, axis=1)


def solve_columns(columns, blocks, inverses, width):
    out = []
    for k in range(PANELS):
        part = columns[k * width : (k + 1) * width]
        for m in range(k):
            part = part - mm(blocks[k, m], out[m])
        out.append(mm(inverses[k], part))
    return jnp.concatenate(out, axis=0)


def shards(matrix, checksum, failed):
    rows_count = lax.axis_size("row")
    cols_count = lax.axis_size(COL)
    p = lax.axis_index("row")
    q = lax.axis_index(COL)
    tr, width, tc = (matrix.shape[1], matrix.shape[2], matrix.shape[4])
    tiles = matrix.reshape(tr, width, tc, width)
    checks = checksum.reshape(tr, width, tc, width)
    piece = width // cols_count
    missing = gather_by_exchange(failed, COL).reshape(-1)[0]

    first = tiles[:, :, 0, :].reshape(tr, cols_count, piece, width).transpose(1, 0, 2, 3)
    parts = lax.all_to_all(first, COL, 0, 0, tiled=True)
    members = jnp.arange(cols_count)[:, None, None, None]
    healthy = jnp.sum(jnp.where(members != missing, parts, 0.0), axis=0)
    check_piece = lax.dynamic_slice_in_dim(checks, q * piece, piece, 1)
    rebuilt = check_piece[:, :, 0, :] - healthy
    panel_piece = jnp.concatenate(
        [jnp.where(missing == k, rebuilt, parts[k]) for k in range(PANELS)], axis=-1
    )

    both = jnp.stack([panel_piece[0], check_piece[0].reshape(piece, tc * width)])
    both = gather_by_exchange(both, "row")[:PANELS]
    lead = gather_by_exchange(both[:, 0], COL)
    lead = lead.transpose(1, 0, 2, 3).reshape(PANELS * width, PANELS * width)
    top = lax.all_gather(both[:, 1], COL)
    top = top.transpose(1, 0, 2, 3).reshape(PANELS * width, tc * width)

    row_panel = lax.all_gather(panel_piece, COL)
    row_panel = row_panel.transpose(1, 0, 2, 3).reshape(tr * width, PANELS * width)
    swap = [(i * cols_count + j, j * cols_count + i) for i in range(rows_count) for j in range(cols_count)]
    col_piece = lax.ppermute(panel_piece, ("row",) + COL, swap)
    col_panel = lax.all_gather(col_piece, "row")
    col_panel = col_panel.transpose(1, 0, 2, 3).reshape(tc * width, PANELS * width)

    lower = [(a, b) for a in range(tr) for b in range(min(a + 1, tc))]
    stacked = jnp.stack([tiles[a, :, b, :] for a, b in lower])
    others = lax.psum(jnp.where(q != missing, stacked, 0.0), COL)
    held = jnp.stack([checks[a, :, b, :] for a, b in lower]) - others
    work = jnp.where(q == missing, held, stacked)

    blocks, inverses = factor_lead(lead, width)
    x_rows = solve_rows(row_panel, blocks, inverses, width)
    x_cols = solve_rows(col_panel, blocks, inverses, width)
    sums = solve_columns(top, blocks, inverses, width)

    totals = checks.reshape(tr * width, tc * width) - mm(x_rows, sums)

    triangle = jnp.tril(jnp.ones((width, width), jnp.bool_))
    zero = jnp.zeros((width, width), jnp.float32)
    columns = [[zero] * tr for _ in range(tc)]
    for n, (a, b) in enumerate(lower):
        i, j = p + a * rows_count, q + b * cols_count
        x_a = x_rows[a * width : (a + 1) * width]
        tile = work[n] - mm_t(x_a, x_cols[b * width : (b + 1) * width])
        for k in range(b * cols_count, min(PANELS, (b + 1) * cols_count)):
            own = x_a[:, k * width : (k + 1) * width]
            own = jnp.where(jnp.logical_or(i > k, triangle), own, 0.0)
            tile = jnp.where(j == k, own, tile)
        columns[b][a] = jnp.where(i >= j, tile, 0.0)
    factored = jnp.stack([jnp.stack(c, axis=0) for c in columns], axis=2)
    return (factored.reshape(matrix.shape), totals.reshape(checksum.shape))


def solution(mesh):
    finer = Mesh(mesh.devices.reshape(mesh.shape["row"], 2, 8), ("row", "col_0", "col_1"))
    in_specs = (P("row", None, None, COL, None, None), P("row", None, None, None, None), P(COL))
    out_specs = (P("row", None, None, COL, None, None), P("row", None, None, None, None))
    return jax.shard_map(
        shards, mesh=finer, in_specs=in_specs, out_specs=out_specs, check_vma=False
    )
```

time: 1410 us -> 615 us (0.44)
  waiting for transfers between devices: 1100 us -> 248 us
  matrix products: 19.2 us -> 50.5 us
  starting transfers between devices: 10.8 us -> 35.3 us
  local copies, waits for them, and re-layouts: 54.7 us -> 73 us
  other arithmetic: 194 us -> 178 us
    psum x8 -> x1, waiting for transfers between devices: 646 us -> 89.2 us  [shards(): others = lax.psum(jnp.where(q != missing, stacked, 0.0), COL)]
    all_gather x6 -> x3, waiting for transfers between devices: 450 us -> 121 us  [the longest x1 70.3 us: shards(): row_panel = lax.all_gather(panel_piece, COL)]
    dot_general x3 -> x32, matrix products: 11.6 us -> 44.6 us  [the longest x25 32.2 us: mm_t(): return lax.dot_general(a, b, (((1,), (1,)), ((), ())), precision=HIGHEST)]
    all_to_all x1 -> x4, waiting for transfers between devices: 1.49 us -> 22.9 us  [the longest x1 11.6 us: shards(): parts = lax.all_to_all(first, COL, 0, 0, tiled=True)]
    all_to_all x1 -> x4, starting transfers between devices: 9.94 us -> 29.9 us  [the longest x3 21.8 us: gather_by_exchange(): lax.all_to_all(jnp.broadcast_to(x[None], (peers, *x.shape)), axis, 0, 0,...]
    ppermute x0 -> x1, waiting for transfers between devices: none -> 15.1 us  [shards(): col_piece = lax.ppermute(panel_piece, ('row',) + COL, swap)]
    unnamed x23 -> x67, local copies, waits for them, and re-layouts: 24.4 us -> 34.6 us
    another operation x24 -> x30, other arithmetic: 175 us -> 166 us  [the longest x20 105 us: factor_lead(): factor = jnp.linalg.cholesky(blocks[k, k])]
  transfers between devices with their start and end apart: 15 -> 9, of which waited for: 15 -> 6; matrix products, arithmetic and copies ran while one was open for 2% -> 45% of each run, Pallas kernels for 0% -> 0%
where the time goes in v1:
time: 615 us; the launch traced here: 608 us
  waiting for transfers between devices  248 us (40%)
  other arithmetic  178 us (29%)
  local copies, waits for them, and re-layouts  73 us (12%)
  matrix products  50.5 us (8%)
  starting transfers between devices  35.3 us (6%)
  between operations  22.9 us (4%)
    another operation x20, other arithmetic, factor_lead(): factor = jnp.linalg.cholesky(blocks[k, k])  105 us
    psum x1, waiting for transfers between devices, shards(): others = lax.psum(jnp.where(q != missing, stacked, 0.0), COL)  89.2 us
    all_gather x1, waiting for transfers between devices, shards(): row_panel = lax.all_gather(panel_piece, COL)  70.3 us
    another operation x7, other arithmetic, factor_lead(): inverse = jax.scipy.linalg.solve_triangular(factor, eye, lower=True)  60.9 us
    all_gather x1, waiting for transfers between devices, shards(): col_panel = lax.all_gather(col_piece, 'row')  50.5 us
    unnamed x67, local copies, waits for them, and re-layouts  34.6 us
    dot_general x25, matrix products, mm_t(): return lax.dot_general(a, b, (((1,), (1,)), ((), ())), precision=HIGHEST)  32.2 us
    all_to_all x3, starting transfers between devices, gather_by_exchange(): lax.all_to_all(jnp.broadcast_to(x[None], (peers, *x.shape)), axis, 0, 0,...  21.8 us
  transfers between devices with their start and end apart: 9, of which 6 were waited for; matrix products, arithmetic and copies ran while one was open for 45% of the time, Pallas kernels for 0%

profile of v1, /device:TPU:30, one launch (start us, length us, event | category | flops | bytes accessed | tf_op | source)
XLA Modules:
  0.0 607.6 jit_solution(6634952954921494909)
XLA Ops:
  8.4 9.9 %all-to-all-start = ((s32[16,1,1]{2,1,0:T(1,128)}), s32[16,1,1]{2,1,0:T(1,128)S(1)}, u32[]{:S(2)}, u32[]{:S(2)}) async-start(s32[16,1,1]{2,1,0:T(1,128)} %broadcast_in_dim.62), calls=%async_computation | async-start | bytes 16384 | tf_op jit(solution)/shard_map/all_to_all | solution.py:14
  18.4 5.5 copy.73
  25.5 1.4 copy.74
  30.7 8.1 %all-to-all-start.1 = ((f32[16,3,16,256]{3,2,1,0:T(8,128)}), f32[16,3,16,256]{3,2,1,0:T(8,128)S(1)}, u32[]{:S(2)}, u32[]{:S(2)}) async-start(f32[16,3,16,256]{3,2,1,0:T(8,128)} %bitcast.301), calls=%async_computation.1 | async-start | bytes 1572864 | tf_op jit(solution)/shard_map/all_to_all | solution.py:74
  40.9 2.9 broadcast_select_fusion
  46.8 11.6 %all-to-all-done.1 = f32[16,3,16,256]{3,2,1,0:T(8,128)S(1)} async-done(((f32[16,3,16,256]{3,2,1,0:T(8,128)}), f32[16,3,16,256]{3,2,1,0:T(8,128)S(1)}, u32[]{:S(2)}, u32[]{:S(2)}) %all-to-all-start.1) | async-done | bytes 786464 | tf_op jit(solution)/shard_map/all_to_all | solution.py:74
  61.4 7.2 %all-to-all-start.2 = ((f32[16,2,16,768]{3,2,1,0:T(8,128)}), f32[16,2,16,768]{3,2,1,0:T(8,128)}, u32[]{:S(2)}, u32[]{:S(2)}) async-start(f32[16,2,16,768]{3,2,1,0:T(8,128)} %broadcast_in_dim.65), calls=%async_computation.2 | async-start | bytes 3145728 | tf_op jit(solution)/shard_map/all_to_all | solution.py:14
  68.7 5.3 collective-permute-start
  74.0 15.1 %collective-permute-done = f32[3,16,768]{2,1,0:T(8,128)S(1)} collective-permute-done((f32[3,16,768]{2,1,0:T(8,128)S(1)}, f32[3,16,768]{2,1,0:T(8,128)S(1)}, u32[]{:S(2)}, u32[]{:S(2)}) %collective-permute-start) | collective-permute-done | bytes 147488 | tf_op jit(solution)/shard_map/ppermute | solution.py:93
  89.7 11.3 %all-to-all-done.2 = f32[16,2,16,768]{3,2,1,0:T(8,128)} async-done(((f32[16,2,16,768]{3,2,1,0:T(8,128)}), f32[16,2,16,768]{3,2,1,0:T(8,128)}, u32[]{:S(2)}, u32[]{:S(2)}) %all-to-all-start.2) | async-done | bytes 1572896 | tf_op jit(solution)/shard_map/all_to_all | solution.py:14
  101.0 1.7 fusion.126
  102.7 1.7 broadcast_in_dim.67
  104.4 4.7 all-to-all-start.3
  109.1 2.1 copy.88
  111.3 3.3 copy.96
  114.6 2.0 copy.111
  121.7 89.2 %all-reduce.4.cloned.1.call-done = f32[6,256,256]{1,2,0:T(8,128)} async-done(((f32[6,256,256]{1,2,0:T(8,128)}), f32[6,256,256]{1,2,0:T(8,128)}) %all-reduce.4.cloned.1.call-update) | async-done | bytes 1572880 | tf_op jit(solution)/shard_map/psum | solution.py:99
  210.9 3.4 subtract_select_fusion
  214.3 70.3 %all-gather.7.cloned.1.call-done = f32[48,16,768]{2,1,0:T(8,128)} async-done(((f32[3,16,768]{2,1,0:T(8,128)}), f32[48,16,768]{2,1,0:T(8,128)}) %all-gather.7.cloned.1.call-update) | async-done | bytes 2359312 | tf_op jit(solution)/shard_map/all_gather | solution.py:90
  284.6 3.3 copy.76
  287.9 50.5 %all-gather.9.cloned.1.call-done = f32[48,16,768]{2,1,0:T(8,128)} async-done(((f32[3,16,768]{2,1,0:T(8,128)}), f32[48,16,768]{2,1,0:T(8,128)}) %all-gather.9.cloned.1.call-update) | async-done | bytes 2359312 | tf_op jit(solution)/shard_map/all_gather | solution.py:94
  338.4 3.3 copy.89
  341.6 1.8 copy.78
  344.7 11.7 %cholesky.172 = f32[128,128]{1,0:T(8,128)S(1)} custom-call(f32[128,128]{1,0:T(8,128)S(1)} %cholesky.270), custom_call_target="Cholesky" | custom-call | tf_op jit(solution)/shard_map/jit(cholesky)/cholesky | solution.py:31
  356.5 9.8 %custom-call.15 = f32[1,128,128]{1,2,0:T(8,128)S(1)} custom-call(f32[1,128,128]{2,1,0:T(8,128)S(1)} %get-tuple-element.87), custom_call_target="InvertDiagBlocksLowerTriangular" | custom-call | tf_op jit(solution)/shard_map/jit(cholesky)/cholesky | solution.py:31
  366.8 12.2 %cholesky.189 = f32[128,128]{1,0:T(8,128)S(1)} custom-call(f32[128,128]{1,0:T(8,128)S(1)} %convolution_subtract_fusion.22), custom_call_target="Cholesky" | custom-call | tf_op jit(solution)/shard_map/jit(cholesky)/cholesky | solution.py:31
  381.1 4.1 while.6
  385.2 19.7 %custom-call.16 = f32[2,128,128]{1,2,0:T(8,128)S(1)} custom-call(f32[2,128,128]{2,1,0:T(8,128)S(1)} %get-tuple-element.24), custom_call_target="InvertDiagBlocksLowerTriangular" | custom-call | tf_op jit(solution)/shard_map/jit(_solve_triangular)/triangular_solve | solution.py:32
  406.6 2.0 fusion.32
  408.6 2.3 fusion.127
  410.9 1.4 convolution_subtract_fusion.15
  412.2 2.3 fusion.128
  415.3 11.7 %cholesky.206 = f32[128,128]{1,0:T(8,128)S(1)} custom-call(f32[128,128]{1,0:T(8,128)S(1)} %cholesky.273), custom_call_target="Cholesky" | custom-call | tf_op jit(solution)/shard_map/jit(cholesky)/cholesky | solution.py:31
  427.1 9.8 %custom-call.17 = f32[1,128,128]{1,2,0:T(8,128)S(1)} custom-call(f32[1,128,128]{2,1,0:T(8,128)S(1)} %get-tuple-element.83), custom_call_target="InvertDiagBlocksLowerTriangular" | custom-call | tf_op jit(solution)/shard_map/jit(cholesky)/cholesky | solution.py:31
  437.5 11.7 %cholesky.223 = f32[128,128]{1,0:T(8,128)S(1)} custom-call(f32[128,128]{1,0:T(8,128)S(1)} %convolution_subtract_fusion.21), custom_call_target="Cholesky" | custom-call | tf_op jit(solution)/shard_map/jit(cholesky)/cholesky | solution.py:31
  452.1 4.3 while.7
  452.8 1.5 bitcast_dynamic-update-slice_fusion.7
  454.9 1.5 bitcast_dynamic-update-slice_fusion.7
  456.4 19.7 %custom-call.18 = f32[2,128,128]{1,2,0:T(8,128)S(1)} custom-call(f32[2,128,128]{2,1,0:T(8,128)S(1)} %get-tuple-element.25), custom_call_target="InvertDiagBlocksLowerTriangular" | custom-call | tf_op jit(solution)/shard_map/jit(_solve_triangular)/triangular_solve | solution.py:32
  477.0 2.3 fusion.31
  483.3 11.7 %cholesky.240 = f32[128,128]{1,0:T(8,128)S(1)} custom-call(f32[128,128]{1,0:T(8,128)S(1)} %cholesky.276), custom_call_target="Cholesky" | custom-call | tf_op jit(solution)/shard_map/jit(cholesky)/cholesky | solution.py:31
  495.1 10.4 %custom-call.19 = f32[1,128,128]{1,2,0:T(8,128)} custom-call(f32[1,128,128]{2,1,0:T(8,128)S(1)} %get-tuple-element.79), custom_call_target="InvertDiagBlocksLowerTriangular" | custom-call | tf_op jit(solution)/shard_map/jit(cholesky)/cholesky | solution.py:31
  507.7 12.1 %cholesky.257 = f32[128,128]{1,0:T(8,128)S(1)} custom-call(f32[128,128]{1,0:T(8,128)S(1)} %convolution_subtract_fusion.20), custom_call_target="Cholesky" | custom-call | tf_op jit(solution)/shard_map/jit(cholesky)/cholesky | solution.py:31
  523.3 4.2 while.8
  523.9 1.4 bitcast_dynamic-update-slice_fusion.8
  526.0 1.4 bitcast_dynamic-update-slice_fusion.8
  528.1 20.5 %custom-call.20 = f32[2,128,128]{1,2,0:T(8,128)S(1)} custom-call(f32[2,128,128]{2,1,0:T(8,128)} %copy-done.23), custom_call_target="InvertDiagBlocksLowerTriangular" | custom-call | tf_op jit(solution)/shard_map/jit(_solve_triangular)/triangular_solve | solution.py:32
  549.8 2.8 convolution_subtract_fusion.3
  554.0 1.5 copy-done.1
  556.3 1.4 convolution_subtract_fusion.5
  558.6 1.4 convolution_subtract_fusion.6
  560.1 1.4 convolution_subtract_fusion.4
  563.8 1.4 fusion.29
  565.3 1.7 fusion.26
  567.0 1.5 fusion.22
  568.5 1.5 fusion.18
  570.1 1.4 fusion.28
  571.6 1.5 fusion.27
  573.2 1.6 maximum_bitcast_fusion
  574.7 6.8 %copy.97 = f32[1,3,256,1,3,256]{5,3,4,2,1,0:T(1,128)} copy(f32[1,3,256,1,3,256]{2,5,1,4,3,0:T(8,128)} %maximum_bitcast_fusion) | data formatting | bytes 4718592
  581.6 1.8 fusion.124
  588.5 7.4 %fusion.6 = f32[768,768]{1,0:T(8,128)} fusion(f32[768,768]{1,0:T(8,128)S(1)} %bitcast.288, f32[256,768]{1,0:T(8,128)S(1)} %fusion.76, f32[256,768]{1,0:T(8,128)S(1)} %fusion.79, f32[256,768]{1,0:T(8,128)S(1)} %fusion.88, f32[768,256]{0,1:T(8,128)S(1)} %fusion.78, f32[768,256]{0,1:T(8,128)S(1)} %fusion.81, f32[768,256]{0,1:T(8,128)S(1)} %fusion.35), kind=kOutput, calls=%fused_computation.15 | convolution fusion | flops 5438767104 | bytes 9437184 | tf_op jit(solution)/shard_map/dot_general | solution.py:18
  595.9 3.1 reshape.70
  599.0 1.8 copy.98
  (171 shorter events, 52.0 us)
Async XLA Ops:
  8.4 22.3 %all-to-all-start = ((s32[16,1,1]{2,1,0:T(1,128)}), s32[16,1,1]{2,1,0:T(1,128)S(1)}, u32[]{:S(2)}, u32[]{:S(2)}) async-start(s32[16,1,1]{2,1,0:T(1,128)} %broadcast_in_dim.62), calls=%async_computation | async-start | bytes 16384 | tf_op jit(solution)/shard_map/all_to_all | solution.py:14
  30.7 27.6 %all-to-all-start.1 = ((f32[16,3,16,256]{3,2,1,0:T(8,128)}), f32[16,3,16,256]{3,2,1,0:T(8,128)S(1)}, u32[]{:S(2)}, u32[]{:S(2)}) async-start(f32[16,3,16,256]{3,2,1,0:T(8,128)} %bitcast.301), calls=%async_computation.1 | async-start | bytes 1572864 | tf_op jit(solution)/shard_map/all_to_all | solution.py:74
  38.9 172.0 %all-reduce.4.cloned.1.call-start = ((), (), s32[]{:S(2)}) async-start(), calls=%async_computation.4 | async-start | bytes 3145728 | tf_op jit(solution)/shard_map/psum | solution.py:99
  40.9 3.0 copy-start
  43.9 240.7 %all-gather.7.cloned.1.call-start = ((), (), s32[]{:S(2)}) async-start(), calls=%async_computation.5 | async-start | bytes 2506752 | tf_op jit(solution)/shard_map/all_gather | solution.py:90
  60.1 8.6 %copy-start.19 = (f32[3,16,768]{2,1,0:T(8,128)S(1)}, f32[3,16,768]{2,1,0:T(8,128)}, u32[]{:S(2)}) copy-start(f32[3,16,768]{2,1,0:T(8,128)} %pad_maximum_fusion.8) | copy-start | bytes 442372
  61.4 39.6 %all-to-all-start.2 = ((f32[16,2,16,768]{3,2,1,0:T(8,128)}), f32[16,2,16,768]{3,2,1,0:T(8,128)}, u32[]{:S(2)}, u32[]{:S(2)}) async-start(f32[16,2,16,768]{3,2,1,0:T(8,128)} %broadcast_in_dim.65), calls=%async_computation.2 | async-start | bytes 3145728 | tf_op jit(solution)/shard_map/all_to_all | solution.py:14
  68.6 269.7 %all-gather.9.cloned.1.call-start = ((), (), s32[]{:S(2)}) async-start(), calls=%async_computation.6 | async-start | bytes 2506752 | tf_op jit(solution)/shard_map/all_gather | solution.py:94
  68.7 20.4 %collective-permute-start = (f32[3,16,768]{2,1,0:T(8,128)S(1)}, f32[3,16,768]{2,1,0:T(8,128)S(1)}, u32[]{:S(2)}, u32[]{:S(2)}) collective-permute-start(f32[3,16,768]{2,1,0:T(8,128)S(1)} %copy-done.19), channel_id=1, source_target_pairs={{0,0},{1,16},{2,32},{3,48},{4,64},{5,80},{6,96},{7,112},{8,128},{9... | collective-permute-start | bytes 442376 | tf_op jit(solution)/shard_map/ppermute | solution.py:93
  89.1 0.7 copy-start.20
  104.4 237.2 %all-to-all-start.3 = ((f32[16,3,16,768]{3,2,1,0:T(8,128)}), f32[16,3,16,768]{3,2,1,0:T(8,128)}, u32[]{:S(2)}, u32[]{:S(2)}) async-start(f32[16,3,16,768]{3,2,1,0:T(8,128)} %broadcast_in_dim.67), calls=%async_computation.3 | async-start | bytes 4718592 | tf_op jit(solution)/shard_map/all_to_all | solution.py:14
  109.0 472.5 %all-gather.11.cloned.1.call-start = ((), (), s32[]{:S(2)}) async-start(), calls=%async_computation.7 | async-start | bytes 2506752 | tf_op jit(solution)/shard_map/all_gather | solution.py:87
  114.6 2.1 copy-start.5
  116.6 94.3 %copy-start.4 = (f32[6,256,256]{1,2,0:T(8,128)S(1)}, f32[6,256,256]{1,2,0:T(8,128)}, u32[]{:S(2)}) copy-start(f32[6,256,256]{1,2,0:T(8,128)} %fusion.47) | copy-start | bytes 4718596
  116.6 359.8 %copy-start.7 = (f32[256,256]{1,0:T(8,128)}, f32[256,256]{1,0:T(8,128)S(1)}, u32[]{:S(2)}) copy-start(f32[256,256]{1,0:T(8,128)S(1)} %fusion.75) | copy-start | bytes 786436
  343.5 62.7 %copy-start.3 = (f32[16,3,16,768]{3,2,0,1:T(8,128)}, f32[16,3,16,768]{3,2,0,1:T(8,128)S(1)}, u32[]{:S(2)}) copy-start(f32[16,3,16,768]{3,2,0,1:T(8,128)S(1)} %copy.78) | copy-start | bytes 7077892
  408.6 5.9 copy-start.16
  456.4 23.3 %copy-start.15 = (f32[256,256]{1,0:T(8,128)S(1)}, f32[256,256]{1,0:T(8,128)}, u32[]{:S(2)}) copy-start(f32[256,256]{1,0:T(8,128)} %get-tuple-element.68) | copy-start | bytes 786436
  477.0 80.7 %copy-start.11 = (f32[128,256]{1,0:T(8,128)}, f32[128,256]{1,0:T(8,128)S(1)}, u32[]{:S(2)}) copy-start(f32[128,256]{1,0:T(8,128)S(1)} %fusion.94) | copy-start | bytes 393220
  480.3 68.9 %copy-start.8 = (f32[256,256]{1,0:T(8,128)S(1)}, f32[256,256]{1,0:T(8,128)}, u32[]{:S(2)}) copy-start(f32[256,256]{1,0:T(8,128)} %copy-done.7) | copy-start | bytes 786436
  482.6 0.7 copy-start.18
  520.4 1.8 copy-start.17
  527.4 0.7 copy-start.23
  548.6 0.7 copy-start.21
  549.5 11.9 %copy-start.9 = (f32[128,256]{1,0:T(8,128)}, f32[128,256]{1,0:T(8,128)S(1)}, u32[]{:S(2)}) copy-start(f32[128,256]{1,0:T(8,128)S(1)} %fusion.82) | copy-start | bytes 393220
  549.6 3.1 copy-start.22
  553.0 8.5 %copy-start.13 = (f32[128,256]{1,0:T(8,128)}, f32[128,256]{1,0:T(8,128)S(1)}, u32[]{:S(2)}) copy-start(f32[128,256]{1,0:T(8,128)S(1)} %fusion.90) | copy-start | bytes 393220
  553.8 1.7 copy-start.1
  562.4 1.4 copy-start.6
  584.2 1.7 copy-start.12
  585.9 1.7 copy-start.10
  585.9 1.7 copy-start.14
  586.8 1.7 copy-start.2
Sparse Core Ops, SparseCore 0:
  44.0 166.8 all-reduce.3
  212.8 71.7 all-gather.6
  287.6 50.6 all-gather.8
  340.1 72.6 all-gather.10

commit v2 on v0

v2 whole, which is shorter than its diff:
```python
import jax
import jax.numpy as jnp
from jax import lax
from jax.experimental import pallas as pl
from jax.experimental.pallas import tpu as pltpu
from jax.sharding import Mesh
from jax.sharding import PartitionSpec as P

PANELS = 3
COL = ("col_0", "col_1")
LOWER = [(0, 0), (1, 0), (1, 1), (2, 0), (2, 1), (2, 2)]
F32 = jnp.float32
VMEM = pl.BlockSpec(memory_space=pltpu.VMEM)
SMEM = pl.BlockSpec(memory_space=pltpu.SMEM)
PARAMS = pltpu.CompilerParams(vmem_limit_bytes=48 << 20)


def mm(a, b):
    return lax.dot_general(
        a, b, (((1,), (0,)), ((), ())), precision=lax.Precision.HIGHEST, preferred_element_type=F32
    )


def mm_t(a, b):
    return lax.dot_general(
        a, b, (((1,), (1,)), ((), ())), precision=lax.Precision.HIGHEST, preferred_element_type=F32
    )


def base_inverse(a):
    n = a.shape[0]
    groups = n // 8
    rows = lax.broadcasted_iota(jnp.int32, (8, n), 0)
    lanes = lax.broadcasted_iota(jnp.int32, (8, n), 1)
    ag = [a[8 * g : 8 * g + 8, :] for g in range(groups)]
    mg = [jnp.where(lanes == rows + 8 * g, 1.0, 0.0).astype(F32) for g in range(groups)]
    for m in range(groups):
        columns = [
            [
                jnp.broadcast_to(ag[g][:, 8 * m + k : 8 * m + k + 1], (8, n))
                for g in range(m, groups)
            ]
            for k in range(8)
        ]
        top, mine = ag[m], mg[m]
        us, vs, ls = [], [], []
        for k in range(8):
            scale = lax.rsqrt(columns[k][0][k : k + 1, :])
            l = [x * scale for x in columns[k]]
            for k2 in range(k + 1, 8):
                s = l[0][k2 : k2 + 1, :]
                columns[k2] = [x - y * s for x, y in zip(columns[k2], l)]
            u = top[k : k + 1, :] * scale
            v = mine[k : k + 1, :] * scale
            below = jnp.where(rows > k, l[0], 0.0)
            top = top - below * u
            mine = jnp.where(rows == k, v, mine - below * v)
            us.append(u)
            vs.append(v)
            ls.append(l[1:])
        mg[m] = mine
        for t, g in enumerate(range(m + 1, groups)):
            ag[g] = ag[g] - sum(ls[k][t] * us[k] for k in range(8))
            mg[g] = mg[g] - sum(ls[k][t] * vs[k] for k in range(8))
    return jnp.concatenate(mg, axis=0)


def tile_inverse(a):
    h = a.shape[0] // 2
    first = base_inverse(a[:h, :h])
    l10 = mm_t(a[h:, :h], first)
    second = base_inverse(a[h:, h:] - mm_t(l10, l10))
    low = -mm(second, mm(l10, first))
    return jnp.concatenate(
        [
            jnp.concatenate([first, jnp.zeros_like(first)], 1),
            jnp.concatenate([low, second], 1),
        ],
        0,
    )


def whole(ref, n):
    t = ref[:, n]
    return t.reshape(t.shape[0] * t.shape[1], t.shape[2])


def lead_kernel(t_ref, off_ref, inv_ref):
    tile = lambda n: whole(t_ref, n)
    i0 = tile_inverse(tile(0))
    inv_ref[0] = i0
    l10 = mm_t(tile(1), i0)
    off_ref[0] = l10
    i1 = tile_inverse(tile(2) - mm_t(l10, l10))
    inv_ref[1] = i1
    l20 = mm_t(tile(3), i0)
    off_ref[1] = l20
    l21 = mm_t(tile(4) - mm_t(l20, l10), i1)
    off_ref[2] = l21
    inv_ref[2] = tile_inverse(tile(5) - mm_t(l20, l20) - mm_t(l21, l21))


def tile_rows(a, b, half):
    return pl.ds(a * 1536 + 2 * b + half, 256, stride=6)


def prepare_kernel(m_ref, c_ref, f_ref, col_ref, row_ref):
    for n, (a, b) in enumerate(LOWER):
        for half in range(2):
            lanes = slice(128 * half, 128 * half + 128)
            v = m_ref[tile_rows(a, b, half), :].reshape(16, 16, 128)
            col_ref[:, 16 * n : 16 * n + 16, lanes] = v
            if n == 0:
                row_ref[:, 0:16, lanes] = v
    col_ref[:, 96:104, :] = jnp.full((16, 8, 256), f_ref[0].astype(F32))
    for b in range(3):
        row_ref[:, 16 * b + 16 : 16 * b + 32, :] = c_ref[0, b].reshape(16, 16, 256)


def fix_lead_kernel(g_ref, r_ref, out_ref):
    missing = g_ref[0, 48:49, :]
    rebuilt = []
    for i in range(PANELS):
        part = slice(16 * i, 16 * i + 16)
        healthy = jnp.zeros((16, 256), F32)
        for j in range(16):
            healthy = healthy + jnp.where(missing != float(j), g_ref[j, part, :], 0.0)
        rebuilt.append(r_ref[i, 16:32, :] - healthy)
    for n, (i, k) in enumerate(LOWER):
        v = jnp.where(missing == float(k), rebuilt[i], g_ref[k, 16 * i : 16 * i + 16, :])
        for s in range(16):
            out_ref[s, n] = v


def fix_columns_kernel(g_ref, c_ref, send_ref, panel_ref, lost_ref):
    missing = g_ref[0, 96:97, :]
    for n, (a, b) in enumerate(LOWER):
        part = slice(16 * n, 16 * n + 16)
        healthy = jnp.zeros((16, 256), F32)
        for j in range(16):
            healthy = healthy + jnp.where(missing != float(j), g_ref[j, part, :], 0.0)
        rebuilt = c_ref[a, b] - healthy
        lost_ref[n] = rebuilt
        if b == 0:
            for k in range(PANELS):
                v = jnp.where(missing == float(k), rebuilt, g_ref[k, part, :])
                panel_ref[3 * a + k] = v
                for s in range(16):
                    send_ref[s, 3 * a + k] = v


def finish_kernel(
    place_ref, r_ref, q_ref, k_ref, d_ref, m_ref, c_ref, off_ref, inv_ref,
    f_ref, t_ref, x_ref, y_ref, s_ref,
):
    p, q, missing = place_ref[0], place_ref[1], place_ref[2]

    for source, target in ((r_ref, x_ref), (q_ref, y_ref)):

        @pl.loop(0, 3)
        def _(a, source=source, target=target):
            x0 = mm_t(whole(source, 3 * a), inv_ref[0])
            target[a, 0] = x0
            x1 = mm_t(whole(source, 3 * a + 1) - mm_t(x0, off_ref[0]), inv_ref[1])
            target[a, 1] = x1
            rest = whole(source, 3 * a + 2) - mm_t(x0, off_ref[1]) - mm_t(x1, off_ref[2])
            target[a, 2] = mm_t(rest, inv_ref[2])

    @pl.loop(0, 3)
    def _(b):
        s0 = mm(inv_ref[0], whole(k_ref, b))
        s_ref[b, 0] = s0
        s1 = mm(inv_ref[1], whole(k_ref, 3 + b) - mm(off_ref[0], s0))
        s_ref[b, 1] = s1
        rest = whole(k_ref, 6 + b) - mm(off_ref[1], s0) - mm(off_ref[2], s1)
        s_ref[b, 2] = mm(inv_ref[2], rest)

    @pl.loop(0, 9)
    def _(n):
        a, b = n // 3, n % 3
        total = c_ref[a, b]
        for k in range(PANELS):
            total = total - mm(x_ref[a, k], s_ref[b, k])
        t_ref[a, b] = total

    def store(a, b, value):
        for half in range(2):
            f_ref[tile_rows(a, b, half), :] = value[:, 128 * half : 128 * half + 128]

    for n, (a, b) in enumerate(LOWER):
        i, j = p + 16 * a, q + 16 * b
        kept = i >= j
        panel = jnp.logical_and(kept, j < PANELS) if b == 0 else jnp.bool_(False)
        inner = jnp.logical_and(kept, jnp.logical_not(panel))

        @pl.when(jnp.logical_not(kept))
        def _():
            store(a, b, jnp.zeros((256, 256), F32))

        if b == 0:

            @pl.when(panel)
            def _():
                value = x_ref[a, jnp.minimum(q, PANELS - 1)]
                rows = lax.broadcasted_iota(jnp.int32, (256, 256), 0)
                cols = lax.broadcasted_iota(jnp.int32, (256, 256), 1)
                value = jnp.where(jnp.logical_or(rows >= cols, i > q), value, 0.0)
                store(a, b, value)

        @pl.when(inner)
        def _():
            update = mm_t(x_ref[a, 0], y_ref[b, 0])
            update = update + mm_t(x_ref[a, 1], y_ref[b, 1])
            update = update + mm_t(x_ref[a, 2], y_ref[b, 2])

            @pl.when(q == missing)
            def _():
                store(a, b, whole(d_ref, n) - update)

            @pl.when(q != missing)
            def _():
                for half in range(2):
                    rows = tile_rows(a, b, half)
                    f_ref[rows, :] = m_ref[rows, :] - update[:, 128 * half : 128 * half + 128]

    for a, b in ((0, 1), (0, 2), (1, 2)):
        store(a, b, jnp.zeros((256, 256), F32))


def call(kernel, outs, ins, specs=None, scratch=()):
    shapes = [jax.ShapeDtypeStruct(s, F32) for s in outs]
    return pl.pallas_call(
        kernel,
        out_shape=shapes,
        in_specs=specs or [VMEM] * len(ins),
        out_specs=[VMEM] * len(outs),
        scratch_shapes=[pltpu.VMEM(s, F32) for s in scratch],
        compiler_params=PARAMS,
    )(*ins)


def exchange(x, axis):
    return lax.all_to_all(x, axis, 0, 0, tiled=True)


def to_all(x, axis):
    return exchange(jnp.broadcast_to(x[None], (16, *x.shape)), axis)


def shards(matrix, checksum, failed):
    p = lax.axis_index("row")
    q = lax.axis_index(COL)
    block = matrix.reshape(4608, 128)
    checks = checksum.reshape(3, 256, 3, 256).transpose(0, 2, 1, 3)

    col_send, row_send = call(
        prepare_kernel, [(16, 104, 256), (16, 64, 256)], [block, checks, failed], [VMEM, VMEM, SMEM]
    )
    row_got = exchange(row_send, "row")
    col_got = exchange(col_send, COL)

    first = jnp.concatenate(
        [row_got[:PANELS, :16].reshape(48, 256), jnp.full((8, 256), failed[0].astype(F32))]
    )
    first = to_all(first, COL)
    (lead_send,) = call(fix_lead_kernel, [(16, 6, 16, 256)], [first, row_got[:PANELS]])
    lead = exchange(lead_send, "row")

    top = to_all(row_got[:PANELS, 16:].reshape(9, 16, 256), "row")

    check_piece = lax.dynamic_slice_in_dim(checks, q * 16, 16, 2)
    panel_send, panel_piece, lost_piece = call(
        fix_columns_kernel,
        [(16, 9, 16, 256), (9, 16, 256), (6, 16, 256)],
        [col_got, check_piece],
    )
    row_panel = exchange(panel_send, COL)
    swap = [(i * 16 + j, j * 16 + i) for i in range(16) for j in range(16)]
    col_panel = to_all(lax.ppermute(panel_piece, ("row",) + COL, swap), "row")
    lost = lax.all_gather(lost_piece, COL)

    tiles = [(PANELS, 256, 256)] * 2
    off, inv = call(lead_kernel, tiles, [lead])

    missing = col_got[0, 96, 0].astype(jnp.int32)
    place = jnp.stack([p, q, missing]).astype(jnp.int32)
    factored, totals = call(
        finish_kernel,
        [(4608, 128), (3, 3, 256, 256)],
        [place, row_panel, col_panel, top, lost, block, checks, off, inv],
        [SMEM] + [VMEM] * 8,
        [(3, 3, 256, 256)] * 3,
    )
    totals = totals.transpose(0, 2, 1, 3).reshape(checksum.shape)
    return (factored.reshape(matrix.shape), totals)


def solution(mesh):
    finer = Mesh(mesh.devices.reshape(mesh.shape["row"], 2, 8), ("row", "col_0", "col_1"))
    in_specs = (P("row", None, None, COL, None, None), P("row", None, None, None, None), P(COL))
    out_specs = (P("row", None, None, COL, None, None), P("row", None, None, None, None))
    return jax.shard_map(
        shards, mesh=finer, in_specs=in_specs, out_specs=out_specs, check_vma=False
    )
```

time: 1410 us -> 376 us (0.27)
  waiting for transfers between devices: 1100 us -> 150 us
  other arithmetic: 194 us -> 0.08 us
  Pallas kernels: 0 us -> 74.7 us
  blocking collectives: 0 us -> 68.9 us
  local copies, waits for them, and re-layouts: 54.7 us -> 16.5 us
  starting transfers between devices: 10.8 us -> 43.4 us
  matrix products: 19.2 us -> 0 us
    psum x8 -> x0, waiting for transfers between devices: 646 us -> none  [the longest x6 375 us: from_root_2(): x = lax.psum(x, axis)]
    all_gather x6 -> x1, waiting for transfers between devices: 450 us -> 56.5 us  [shards(): lost = lax.all_gather(lost_piece, COL)]
    another operation x24 -> x1, other arithmetic: 175 us -> 0.08 us  [shards(): place = jnp.stack([p, q, missing]).astype(jnp.int32)]
    all_to_all x1 -> x5, waiting for transfers between devices: 1.49 us -> 81.7 us  [exchange(): return lax.all_to_all(x, axis, 0, 0, tiled=True)]
    pallas_call x0 -> x5, Pallas kernels: none -> 74.7 us  [call(): pl.pallas_call(kernel, out_shape=shapes, in_specs=specs or [VMEM] * len(i...]
    all_to_all x0 -> x2, blocking collectives: none -> 68.9 us  [exchange(): return lax.all_to_all(x, axis, 0, 0, tiled=True)]
    all_to_all x1 -> x5, starting transfers between devices: 9.94 us -> 37.4 us  [exchange(): return lax.all_to_all(x, axis, 0, 0, tiled=True)]
    another operation x31 -> x0, local copies, waits for them, and re-layouts: 14.2 us -> none  [the longest x22 12.2 us: solve_panel(): jax.scipy.linalg.solve_triangular(factor, stacked.T, lower=True)]
  transfers between devices with their start and end apart: 15 -> 7, of which waited for: 15 -> 6; matrix products, arithmetic and copies ran while one was open for 2% -> 1% of each run, Pallas kernels for 0% -> 8%
where the time goes in v2:
time: 376 us; the launch traced here: 370 us
  waiting for transfers between devices  150 us (40%)
  Pallas kernels  74.7 us (20%)
  blocking collectives  68.9 us (18%)
  starting transfers between devices  43.4 us (12%)
  local copies, waits for them, and re-layouts  16.5 us (4%)
  between operations  15.9 us (4%)
    all_to_all x5, waiting for transfers between devices, exchange(): return lax.all_to_all(x, axis, 0, 0, tiled=True)  81.7 us
    pallas_call x5, Pallas kernels, call(): pl.pallas_call(kernel, out_shape=shapes, in_specs=specs or [VMEM] * len(i...  74.7 us
    all_to_all x2, blocking collectives, exchange(): return lax.all_to_all(x, axis, 0, 0, tiled=True)  68.9 us
    all_gather x1, waiting for transfers between devices, shards(): lost = lax.all_gather(lost_piece, COL)  56.5 us
    all_to_all x5, starting transfers between devices, exchange(): return lax.all_to_all(x, axis, 0, 0, tiled=True)  37.4 us
    ppermute x1, waiting for transfers between devices, shards(): col_panel = to_all(lax.ppermute(panel_piece, ('row',) + COL, swap), 'row')  11.5 us
    unnamed x22, local copies, waits for them, and re-layouts  10.2 us
  transfers between devices with their start and end apart: 7, of which 6 were waited for; matrix products, arithmetic and copies ran while one was open for 1% of the time, Pallas kernels for 8%

profile of v2, /device:TPU:30, one launch (start us, length us, event | category | flops | bytes accessed | tf_op | source)
XLA Modules:
  0.0 369.8 jit_solution(10286542089971264791)
XLA Ops:
  7.8 0.0 copy-start
  7.8 1.7 copy-done
  9.5 2.8 shard_map.50
  12.3 0.0 copy-start.6
  12.3 1.2 copy-done.6
  13.5 7.2 %all-to-all-start.3 = ((f32[16,64,256]{2,1,0:T(8,128)}), f32[16,64,256]{2,1,0:T(8,128)S(1)}, u32[]{:S(2)}, u32[]{:S(2)}) async-start(f32[16,64,256]{2,1,0:T(8,128)} %get-tuple-element.14), calls=%async_computation.3 | async-start | bytes 2097152 | tf_op jit(solution)/shard_map/all_to_all | solution.py:243
  20.7 13.0 %all-to-all-done.3 = f32[16,64,256]{2,1,0:T(8,128)S(1)} async-done(((f32[16,64,256]{2,1,0:T(8,128)}), f32[16,64,256]{2,1,0:T(8,128)S(1)}, u32[]{:S(2)}, u32[]{:S(2)}) %all-to-all-start.3) | async-done | bytes 1048608 | tf_op jit(solution)/shard_map/all_to_all | solution.py:243
  33.7 0.0 copy-start.10
  33.7 0.1 broadcast_in_dim.11
  33.8 33.1 %all_to_all.35.g_ref = f32[16,56,256]{2,1,0:T(8,128)S(1)} all-to-all(f32[16,56,256]{2,1,0:T(8,128)S(1)} %broadcast_in_dim.11), channel_id=1, replica_groups=mesh['row'=16,'col_0'=2,'col_1'=8] {'col_0','col_1'}, dimensions={0} | all-to-all | bytes 1835008 | tf_op jit(solution)/shard_map/all_to_all | solution.py:243
  66.9 0.0 copy-done.10
  66.9 5.5 %all-to-all-start = ((f32[16,104,256]{2,1,0:T(8,128)}), f32[16,104,256]{2,1,0:T(8,128)S(1)}, u32[]{:S(2)}, u32[]{:S(2)}) async-start(f32[16,104,256]{2,1,0:T(8,128)} %copy-done.6), calls=%async_computation | async-start | bytes 3407872 | tf_op jit(solution)/shard_map/all_to_all | solution.py:243
  72.4 0.9 slice.17
  73.3 37.9 %all-to-all-done.g_ref = f32[16,104,256]{2,1,0:T(8,128)S(1)} async-done(((f32[16,104,256]{2,1,0:T(8,128)}), f32[16,104,256]{2,1,0:T(8,128)S(1)}, u32[]{:S(2)}, u32[]{:S(2)}) %all-to-all-start) | async-done | bytes 1703968 | tf_op jit(solution)/shard_map/all_to_all | solution.py:243
  111.2 0.0 copy-start.1
  111.2 1.9 broadcast_in_dim.10
  113.1 9.0 %all-to-all-start.4 = ((f32[16,9,16,256]{3,2,1,0:T(8,128)}), f32[16,9,16,256]{3,2,1,0:T(8,128)}, u32[]{:S(2)}, u32[]{:S(2)}) async-start(f32[16,9,16,256]{3,2,1,0:T(8,128)} %broadcast_in_dim.10), calls=%async_computation.4 | async-start | bytes 4718592 | tf_op jit(solution)/shard_map/all_to_all | solution.py:243
  122.1 0.9 slice.19.r_ref
  123.1 0.2 shard_map.52
  123.3 0.0 copy-start.4
  123.3 1.2 copy-done.4
  124.4 25.6 %all-to-all-done.4.k_ref = f32[16,9,16,256]{3,2,1,0:T(8,128)} async-done(((f32[16,9,16,256]{3,2,1,0:T(8,128)}), f32[16,9,16,256]{3,2,1,0:T(8,128)}, u32[]{:S(2)}, u32[]{:S(2)}) %all-to-all-start.4) | async-done | bytes 2359328 | tf_op jit(solution)/shard_map/all_to_all | solution.py:243
  150.0 9.8 %all-to-all-start.6 = ((f32[16,6,16,256]{3,2,1,0:T(8,128)}), f32[16,6,16,256]{3,2,1,0:T(8,128)S(1)}, u32[]{:S(2)}, u32[]{:S(2)}) async-start(f32[16,6,16,256]{3,2,1,0:T(8,128)} %copy-done.4), calls=%async_computation.6 | async-start | bytes 3145728 | tf_op jit(solution)/shard_map/all_to_all | solution.py:243
  159.8 0.9 dynamic-slice_bitcast_fusion.c_ref
  160.8 0.0 copy-done.1
  160.8 1.1 shard_map.51
  161.8 0.0 copy-start.5
  161.8 1.4 copy-done.5
  163.2 5.8 %collective-permute-start = (f32[9,16,256]{2,1,0:T(8,128)S(1)}, f32[9,16,256]{2,1,0:T(8,128)S(1)}, u32[]{:S(2)}, u32[]{:S(2)}) collective-permute-start(f32[9,16,256]{2,1,0:T(8,128)S(1)} %get-tuple-element.13), channel_id=1, source_target_pairs={{0,0},{1,16},{2,32},{3,48},{4,64},{5,80},{6,96},{7,112},{8,128},{9... | collective-permute-start | bytes 442376 | tf_op jit(solution)/shard_map/ppermute | solution.py:279
  169.1 11.5 %collective-permute-done = f32[9,16,256]{2,1,0:T(8,128)S(1)} collective-permute-done((f32[9,16,256]{2,1,0:T(8,128)S(1)}, f32[9,16,256]{2,1,0:T(8,128)S(1)}, u32[]{:S(2)}, u32[]{:S(2)}) %collective-permute-start) | collective-permute-done | bytes 147488 | tf_op jit(solution)/shard_map/ppermute | solution.py:279
  180.6 5.2 %all-to-all-done.6.t_ref = f32[16,6,16,256]{3,2,1,0:T(8,128)S(1)} async-done(((f32[16,6,16,256]{3,2,1,0:T(8,128)}), f32[16,6,16,256]{3,2,1,0:T(8,128)S(1)}, u32[]{:S(2)}, u32[]{:S(2)}) %all-to-all-start.6) | async-done | bytes 1572896 | tf_op jit(solution)/shard_map/all_to_all | solution.py:243
  185.9 0.0 copy-start.2
  185.9 0.3 broadcast_in_dim.8
  186.2 35.8 %all_to_all.36.q_ref = f32[16,9,16,256]{3,2,1,0:T(8,128)} all-to-all(f32[16,9,16,256]{3,2,1,0:T(8,128)S(1)} %broadcast_in_dim.8), channel_id=1, replica_groups=mesh['row'=16,'col_0'=2,'col_1'=8] {'row'}, dimensions={0} | all-to-all | bytes 4718592 | tf_op jit(solution)/shard_map/all_to_all | solution.py:243
  221.9 0.0 copy-done.2
  221.9 5.8 %all-to-all-start.1 = ((f32[16,9,16,256]{3,2,1,0:T(8,128)}), f32[16,9,16,256]{3,2,1,0:T(8,128)S(1)}, u32[]{:S(2)}, u32[]{:S(2)}) async-start(f32[16,9,16,256]{3,2,1,0:T(8,128)} %copy-done.5), calls=%async_computation.1 | async-start | bytes 4718592 | tf_op jit(solution)/shard_map/all_to_all | solution.py:243
  227.8 0.2 all-gather.3.cloned.1.call-start
  228.0 0.5 all-gather.3.cloned.1.call-update
  228.5 1.3 slice.16
  230.4 0.1 pad_add_fusion.place_ref
  230.5 0.0 copy-start.3
  230.5 1.4 copy-done.3
  231.9 28.9 %shard_map.53 = (f32[3,256,256]{2,1,0:T(8,128)S(1)}, f32[3,256,256]{2,1,0:T(8,128)S(1)}) custom-call(f32[16,6,16,256]{3,2,1,0:T(8,128)S(1)} %copy-done.3), custom_call_target="tpu_custom_call" | custom-call | tf_op jit(solution)/shard_map/pallas_call | solution.py:232
  260.8 0.0 copy-start.8
  260.8 0.9 copy-done.8
  261.7 56.5 %all-gather.3.cloned.1.call-done = f32[96,16,256]{2,1,0:T(8,128)} async-done(((f32[6,16,256]{2,1,0:T(8,128)}), f32[96,16,256]{2,1,0:T(8,128)}) %all-gather.3.cloned.1.call-update) | async-done | bytes 1572880 | tf_op jit(solution)/shard_map/all_gather | solution.py:280
  318.2 0.0 all-to-all-done.1.r_ref
  318.2 0.0 copy-start.7
  318.2 1.4 copy-done.7
  319.6 0.0 copy-start.9
  319.6 1.1 copy-done.9
  320.8 41.7 %shard_map.54 = (f32[4608,128]{1,0:T(8,128)}, f32[3,3,256,256]{3,2,1,0:T(8,128)}) custom-call(s32[3]{0:T(128)S(1)} %pad_add_fusion.place_ref, f32[16,9,16,256]{3,2,1,0:T(8,128)S(1)} %all-to-all-done.1.r_ref, f32[16,9,16,256]{3,2,1,0:T(8,128)} %all_to_all.36.q_ref, f32[16,9,16,256]{3,2,1,0:T(8,128)} %all-to-all-done.4.k_ref, f32[16,6,16,256]{3,2,1,0:T(8,128)S(1)} %bitcast.21, ...), custom_call_target="tpu_custom_call" | custom-call | tf_op jit(solution)/shard_map/pallas_call | solution.py:232
  (2 shorter events, 0.0 us)
Async XLA Ops:
  7.8 1.7 copy-start
  12.3 1.2 copy-start.6
  13.5 20.2 %all-to-all-start.3 = ((f32[16,64,256]{2,1,0:T(8,128)}), f32[16,64,256]{2,1,0:T(8,128)S(1)}, u32[]{:S(2)}, u32[]{:S(2)}) async-start(f32[16,64,256]{2,1,0:T(8,128)} %get-tuple-element.14), calls=%async_computation.3 | async-start | bytes 2097152 | tf_op jit(solution)/shard_map/all_to_all | solution.py:243
  33.7 33.2 %copy-start.10 = (f32[16,64,256]{2,1,0:T(8,128)}, f32[16,64,256]{2,1,0:T(8,128)S(1)}, u32[]{:S(2)}) copy-start(f32[16,64,256]{2,1,0:T(8,128)S(1)} %all-to-all-done.3) | copy-start | bytes 3145732
  66.9 44.3 %all-to-all-start = ((f32[16,104,256]{2,1,0:T(8,128)}), f32[16,104,256]{2,1,0:T(8,128)S(1)}, u32[]{:S(2)}, u32[]{:S(2)}) async-start(f32[16,104,256]{2,1,0:T(8,128)} %copy-done.6), calls=%async_computation | async-start | bytes 3407872 | tf_op jit(solution)/shard_map/all_to_all | solution.py:243
  111.2 49.6 %copy-start.1 = (f32[16,104,256]{2,1,0:T(8,128)}, f32[16,104,256]{2,1,0:T(8,128)S(1)}, u32[]{:S(2)}) copy-start(f32[16,104,256]{2,1,0:T(8,128)S(1)} %all-to-all-done.g_ref) | copy-start | bytes 5111812
  113.1 36.9 %all-to-all-start.4 = ((f32[16,9,16,256]{3,2,1,0:T(8,128)}), f32[16,9,16,256]{3,2,1,0:T(8,128)}, u32[]{:S(2)}, u32[]{:S(2)}) async-start(f32[16,9,16,256]{3,2,1,0:T(8,128)} %broadcast_in_dim.10), calls=%async_computation.4 | async-start | bytes 4718592 | tf_op jit(solution)/shard_map/all_to_all | solution.py:243
  123.3 1.2 copy-start.4
  150.0 35.8 %all-to-all-start.6 = ((f32[16,6,16,256]{3,2,1,0:T(8,128)}), f32[16,6,16,256]{3,2,1,0:T(8,128)S(1)}, u32[]{:S(2)}, u32[]{:S(2)}) async-start(f32[16,6,16,256]{3,2,1,0:T(8,128)} %copy-done.4), calls=%async_computation.6 | async-start | bytes 3145728 | tf_op jit(solution)/shard_map/all_to_all | solution.py:243
  161.8 1.4 copy-start.5
  163.2 17.4 %collective-permute-start = (f32[9,16,256]{2,1,0:T(8,128)S(1)}, f32[9,16,256]{2,1,0:T(8,128)S(1)}, u32[]{:S(2)}, u32[]{:S(2)}) collective-permute-start(f32[9,16,256]{2,1,0:T(8,128)S(1)} %get-tuple-element.13), channel_id=1, source_target_pairs={{0,0},{1,16},{2,32},{3,48},{4,64},{5,80},{6,96},{7,112},{8,128},{9... | collective-permute-start | bytes 442376 | tf_op jit(solution)/shard_map/ppermute | solution.py:279
  185.9 36.1 %copy-start.2 = (f32[16,6,16,256]{3,2,1,0:T(8,128)}, f32[16,6,16,256]{3,2,1,0:T(8,128)S(1)}, u32[]{:S(2)}) copy-start(f32[16,6,16,256]{3,2,1,0:T(8,128)S(1)} %all-to-all-done.6.t_ref) | copy-start | bytes 4718596
  221.9 96.3 %all-to-all-start.1 = ((f32[16,9,16,256]{3,2,1,0:T(8,128)}), f32[16,9,16,256]{3,2,1,0:T(8,128)S(1)}, u32[]{:S(2)}, u32[]{:S(2)}) async-start(f32[16,9,16,256]{3,2,1,0:T(8,128)} %copy-done.5), calls=%async_computation.1 | async-start | bytes 4718592 | tf_op jit(solution)/shard_map/all_to_all | solution.py:243
  227.8 90.5 %all-gather.3.cloned.1.call-start = ((), (), s32[]{:S(2)}) async-start(), calls=%async_computation.7 | async-start | bytes 1671168 | tf_op jit(solution)/shard_map/all_gather | solution.py:280
  230.5 1.4 copy-start.3
  260.8 0.9 copy-start.8
  318.2 1.4 copy-start.7
  319.6 1.1 copy-start.9
Sparse Core Ops, SparseCore 0:
  230.4 87.8 all-gather.2
